TPU v7x, 32 devices: a whole 2x2x4 slice. The times are simulated.
32 devices in a mesh: ctx: 8 (over z, y), fsdp: 4 (over x, core).
Axes of the slice: x: 2, y: 2, z: 4, core: 2. Of those that a mesh axis runs over, the one named last changes fastest.
Arguments:
- tokens: bfloat16 [4, 2048, 8192], P('fsdp', 'ctx'), may hold values from -6 to 6
- w_query: bfloat16 [8192, 512], P('fsdp'), may hold values from -0.125 to 0.125
- keys: bfloat16 [4, 2048, 128], P('fsdp', 'ctx'), may hold values from -512 to 512
- values: bfloat16 [4, 2048, 128], P('fsdp', 'ctx'), may hold values from -6 to 6
- gates: bfloat16 [4, 2048, 3], P('fsdp', 'ctx'), may hold values from 0.25 to 1
- routes: int32 [4, 2048, 2], P('fsdp', 'ctx'), may hold values from 0 to 2, all different within a row
- w_out: bfloat16 [512, 8192], P(None, 'fsdp'), may hold values from -1 to 1
Outputs:
- mixed: bfloat16 [4, 2048, 8192], P('fsdp', 'ctx')
Inputs may be any that keep to these rules, and one draw needn't show every extreme that they name: `routes`: the 2 routed heads of a token differ.
All inputs are finite; a program needn't handle non-finite values.
Results may differ from a plain program's by a relative error of at most 0.035.
Values may be sent and summed in bfloat16 or wider, within the bound.
A program may use at most 128 MiB of HBM per device.

v0:
```python
import jax
import jax.numpy as jnp
from jax import lax
from jax.sharding import PartitionSpec as P

theta_base = 500000.0


def rotate(projected, positions, head_size):
    tok_rows = projected.shape[0]
    by_head = projected.reshape(tok_rows, -1, head_size)
    middle = head_size // 2
    inv_freq = jnp.power(theta_base, -2.0 * jnp.arange(middle, dtype=jnp.float32) / head_size)
    angles = positions[:, None] * inv_freq[None, :]
    cosine = jnp.cos(angles)[:, None, :]
    sine_part = jnp.sin(angles)[:, None, :]
    front_part = by_head[:, :, :middle]
    back_part = by_head[:, :, middle:]
    turned = jnp.concatenate(
        [front_part * cosine - back_part * sine_part, back_part * cosine + front_part * sine_part],
        axis=2,
    )
    return turned.reshape(tok_rows, -1)


def head_weights(gates, routes, head_count):
    gains = gates.astype(jnp.float32)
    head_index = jnp.arange(head_count, dtype=jnp.int32)[None, :]
    shared = (head_index == 0).astype(jnp.float32) * gains[:, 0:1]
    first_pick = (head_index == routes[:, 0:1] + 1).astype(jnp.float32) * gains[:, 1:2]
    second_pick = (head_index == routes[:, 1:2] + 1).astype(jnp.float32) * gains[:, 2:3]
    return shared + first_pick + second_pick


def per_device(tokens, w_query, keys, values, gates, routes, w_out):
    tok_rows = tokens.shape[1]
    half_rows = tok_rows // 2
    head_size = keys.shape[2]
    head_count = w_query.shape[1] // head_size
    score_scale = head_size ** (-0.5)
    cycle_index = lax.axis_index("ctx")
    x_local = tokens[0]
    projected = jnp.dot(
        x_local,
        lax.all_gather(w_query, "fsdp", axis=0, tiled=True),
        preferred_element_type=jnp.float32,
    )
    own_positions = cycle_index * tok_rows + jnp.arange(tok_rows, dtype=jnp.int32)
    rotated = rotate(projected, own_positions.astype(jnp.float32), head_size).astype(jnp.bfloat16)
    weights = head_weights(gates[0], routes[0], head_count)
    key_value = jnp.concatenate([keys[0], values[0]], axis=1)
    half_range = jnp.arange(half_rows, dtype=jnp.int32)
    query_pos = jnp.concatenate(
        [cycle_index * tok_rows + half_range, cycle_index * tok_rows + half_rows + half_range]
    )
    grouped = (
        rotated.reshape(2, half_rows, head_count, head_size)
        .transpose(0, 2, 1, 3)
        .reshape(2, head_count * half_rows, head_size)
    )
    grouped_pos = jnp.broadcast_to(
        query_pos.reshape(2, 1, half_rows), (2, head_count, half_rows)
    ).reshape(2, head_count * half_rows)
    last_pos = jnp.max(query_pos.reshape(2, half_rows), axis=1)

    def update(carried, block_q, block_qpos, block_kv, block_kpos):
        run_max, run_sum, run_acc = carried
        scores = (
            jnp.einsum(
                "qd,kd->qk", block_q, block_kv[:, :head_size], preferred_element_type=jnp.float32
            )
            * score_scale
        )
        visible = block_kpos[None, :] <= block_qpos[:, None]
        new_max = jnp.maximum(run_max, jnp.max(jnp.where(visible, scores, -1e30), axis=1))
        factor = jnp.exp(run_max - new_max)
        exp_terms = jnp.where(visible, jnp.exp(scores - new_max[:, None]), 0.0)
        run_sum = run_sum * factor + jnp.sum(exp_terms, axis=1)
        soft_weights = exp_terms.astype(jnp.bfloat16)
        run_acc = run_acc * factor[:, None] + jnp.dot(
            soft_weights, block_kv[:, head_size:], preferred_element_type=jnp.float32
        )
        return (new_max, run_sum, run_acc)

    def absorb_block(carried, block_kv, block_kpos):
        key_first = jnp.min(block_kpos)
        halves_out = []
        for q_half in range(2):
            current = (carried[0][q_half], carried[1][q_half], carried[2][q_half])
            halves_out.append(
                lax.cond(
                    key_first > last_pos[q_half],
                    lambda kept: kept,
                    lambda kept: update(
                        kept, grouped[q_half], grouped_pos[q_half], block_kv, block_kpos
                    ),
                    current,
                )
            )
        return (
            jnp.stack([halves_out[0][0], halves_out[1][0]]),
            jnp.stack([halves_out[0][1], halves_out[1][1]]),
            jnp.stack([halves_out[0][2], halves_out[1][2]]),
        )

    initial = (
        jnp.full((2, head_count * half_rows), -1e30, jnp.float32),
        jnp.zeros((2, head_count * half_rows), jnp.float32),
        jnp.zeros((2, head_count * half_rows, head_size), jnp.float32),
    )
    carried = initial
    block_in = lax.all_gather(key_value, "ctx", axis=0, tiled=True)
    piece_rows = block_in.shape[0]
    key_pos = jnp.arange(piece_rows, dtype=jnp.int32)
    blocks = piece_rows // half_rows

    def absorb_one(running, element):
        return (absorb_block(running, element[0], element[1]), None)

    carried, _ = lax.scan(
        absorb_one,
        carried,
        (
            block_in.reshape(blocks, half_rows, block_in.shape[1]),
            key_pos.reshape(blocks, half_rows),
        ),
    )
    final_max, final_sum, final_acc = carried
    attended = (
        (final_acc / final_sum[:, :, None])
        .reshape(2, head_count, half_rows, head_size)
        .transpose(0, 2, 1, 3)
        .reshape(tok_rows, head_count, head_size)
    )
    hidden = (
        (attended * weights[:, :, None])
        .reshape(tok_rows, head_count * head_size)
        .astype(jnp.bfloat16)
    )
    mixed = jnp.dot(
        hidden,
        lax.all_gather(w_out, "fsdp", axis=1, tiled=True),
        preferred_element_type=jnp.float32,
    ).astype(jnp.bfloat16)
    return mixed[None]


def solution(mesh):
    in_specs = (
        P("fsdp", "ctx", None),
        P("fsdp", None),
        P("fsdp", "ctx", None),
        P("fsdp", "ctx", None),
        P("fsdp", "ctx", None),
        P("fsdp", "ctx", None),
        P(None, "fsdp"),
    )
    out_specs = P("fsdp", "ctx", None)
    return jax.shard_map(
        per_device, mesh=mesh, in_specs=in_specs, out_specs=out_specs, check_vma=False
    )
```

profile of v0, /device:TPU:28, one launch (start us, length us, event | category | flops | bytes accessed | tf_op | source)
XLA Modules:
  0.0 224.6 jit_solution(17087423166515086261)
XLA Ops:
  6.5 0.7 all-gather.6.cloned.1.call-update
  7.3 1.5 pad_maximum_fusion.4
  9.7 0.8 slice_add_fusion.1
  11.8 56.3 %all-gather.6.cloned.1.call-done = bf16[8192,512]{1,0:T(8,128)(2,1)} async-done(((bf16[2048,512]{1,0:T(8,128)(2,1)}), bf16[8192,512]{1,0:T(8,128)(2,1)}) %all-gather.6.cloned.1.call-update) | async-done | bytes 8388624 | tf_op jit(solution)/shard_map/all_gather | solution.py:45
  68.2 11.9 %copy.13 = bf16[512,8192]{1,0:T(8,128)(2,1)} copy(bf16[512,8192]{0,1:T(8,128)(2,1)} %bitcast.116) | data formatting | bytes 16777216 | tf_op jit(solution)/shard_map/dot_general | solution.py:43
  80.1 7.0 %fusion.33 = f32[256,4,128]{0,2,1:T(8,128)S(1)} fusion(bf16[4,128,8192]{2,1,0:T(8,128)(2,1)} %bitcast.117, bf16[1,256,8192]{2,1,0:T(8,128)(2,1)} %param.13), kind=kOutput, calls=%fused_computation.52 | convolution fusion | flops 2147483648 | bytes 13107200 | tf_op jit(solution)/shard_map/dot_general | solution.py:43
  87.5 20.8 %all-gather.4.cloned.1.call-done = bf16[2048,256]{1,0:T(8,128)(2,1)} async-done(((bf16[256,256]{1,0:T(8,128)(2,1)}), bf16[2048,256]{1,0:T(8,128)(2,1)}) %all-gather.4.cloned.1.call-update) | async-done | bytes 1048592 | tf_op jit(solution)/shard_map/all_gather | solution.py:112
  108.4 101.0 %while.15 = (s32[]{:T(128)}, f32[2,512]{1,0:T(2,128)S(1)}, f32[2,512]{1,0:T(2,128)S(1)}, f32[2,512,128]{2,1,0:T(8,128)S(1)}, s32[16,128]{1,0:T(8,128)S(1)}, /*in...) while((s32[]{:T(128)}, f32[2,512]{1,0:T(2,128)S(1)}, ...), condition=%wide.region_11.12_spmd.clone, body=%wide.region_1.11_spmd.clone.sunk | while | flops 69079168 | bytes 5371253 | solution.py:120
  112.3 0.9 dynamic-slice_bitcast_fusion.2
  113.2 0.7 conditional.6
  113.9 0.7 conditional.7
  118.7 0.9 dynamic-slice_bitcast_fusion.2
  119.6 0.7 conditional.6
  120.3 0.7 conditional.7
  125.0 0.9 dynamic-slice_bitcast_fusion.2
  125.9 0.7 conditional.6
  131.4 0.9 dynamic-slice_bitcast_fusion.2
  132.3 0.7 conditional.6
  133.0 0.7 conditional.7
  137.8 0.9 dynamic-slice_bitcast_fusion.2
  138.6 0.7 conditional.6
  144.1 0.9 dynamic-slice_bitcast_fusion.2
  145.0 0.7 conditional.6
  145.7 0.7 conditional.7
  150.5 0.9 dynamic-slice_bitcast_fusion.2
  151.4 0.7 conditional.6
  152.1 0.7 conditional.7
  156.8 0.9 dynamic-slice_bitcast_fusion.2
  157.7 0.7 conditional.6
  163.2 0.9 dynamic-slice_bitcast_fusion.2
  164.1 0.7 conditional.6
  169.5 0.9 dynamic-slice_bitcast_fusion.2
  170.4 0.7 conditional.6
  171.1 0.7 conditional.7
  175.9 0.9 dynamic-slice_bitcast_fusion.2
  176.8 0.7 conditional.6
  182.2 0.9 dynamic-slice_bitcast_fusion.2
  183.1 0.7 conditional.6
  188.6 0.9 dynamic-slice_bitcast_fusion.2
  189.5 0.7 conditional.6
  190.2 0.7 conditional.7
  194.9 0.9 dynamic-slice_bitcast_fusion.2
  195.8 0.7 conditional.6
  201.3 0.9 dynamic-slice_bitcast_fusion.2
  202.2 0.7 conditional.6
  207.6 0.9 dynamic-slice_bitcast_fusion.2
  208.5 0.7 conditional.6
  210.3 7.8 %fusion.32 = bf16[1,256,8192]{2,1,0:T(8,128)(2,1)} fusion(bf16[512,8192]{1,0:T(8,128)(2,1)} %all-gather.8.cloned.1.call-done, f32[32,8,4,128]{3,2,1,0:T(4,128)S(1)} %bitcast.120, f32[32,8,4,128]{3,2,1,0:T(4,128)S(1)} %bitcast.119), kind=kOutput, calls=%fused_computation.51 | convolution fusion | flops 2149842944 | bytes 13631488 | tf_op jit(solution)/shard_map/dot_general | solution.py:140
  (368 shorter events, 52.2 us)
Async XLA Ops:
  6.5 61.6 %all-gather.6.cloned.1.call-start = ((), (), s32[]{:S(2)}) async-start(), calls=%async_computation.1 | async-start | bytes 10485760 | tf_op jit(solution)/shard_map/all_gather | solution.py:45
  7.3 101.1 %all-gather.4.cloned.1.call-start = ((), (), s32[]{:S(2)}) async-start(), calls=%async_computation | async-start | bytes 1179648 | tf_op jit(solution)/shard_map/all_gather | solution.py:112
  8.9 201.1 %all-gather.8.cloned.1.call-start = ((), (), s32[]{:S(2)}) async-start(), calls=%async_computation.2 | async-start | bytes 10485760 | tf_op jit(solution)/shard_map/all_gather | solution.py:142
Sparse Core Ops, SparseCore 0:
  8.9 59.2 all-gather.5
  70.3 37.9 all-gather.3
  109.9 59.2 all-gather.7
where the time goes:
time: 226 us; the launch traced here: 225 us
  waiting for transfers between devices  78.6 us (35%)
  loops' own time  44.3 us (20%)
  local copies, waits for them, and re-layouts  38 us (17%)
  matrix products  31.2 us (14%)
  other arithmetic  19.1 us (8%)
  between operations  13.2 us (6%)
    all_gather x1, waiting for transfers between devices, per_device(): lax.all_gather(w_query, 'fsdp', axis=0, tiled=True)  56.3 us
    another operation x1, loops' own time, per_device(): lax.scan(absorb_one, carried, (block_in.reshape(blocks, half_rows, block_...  43 us
    all_gather x1, waiting for transfers between devices, per_device(): block_in = lax.all_gather(key_value, 'ctx', axis=0, tiled=True)  20.8 us
    squeeze x16, local copies, waits for them, and re-layouts, per_device(): lax.scan(absorb_one, carried, (block_in.reshape(blocks, half_rows, block_...  13.6 us
    dot_general x1, local copies, waits for them, and re-layouts, per_device(): jnp.dot(x_local, lax.all_gather(w_query, 'fsdp', axis=0, tiled=True), pre...  11.9 us
    slice x16, local copies, waits for them, and re-layouts, absorb_block(): last_pos[q_half]  10.6 us
    squeeze x16, other arithmetic, per_device(): lax.scan(absorb_one, carried, (block_in.reshape(blocks, half_rows, block_...  10.2 us
    dot_general x31, matrix products, update(): jnp.dot(soft_weights, block_kv[:, head_size:], preferred_element_type=jnp...  10 us
  transfers between devices with their start and end apart: 3, of which 2 were waited for; matrix products, arithmetic and copies ran while one was open for 36% of the time, Pallas kernels for 0%

commit v1 on v0

v1 whole, which is shorter than its diff:
```python
import functools

import jax
import jax.numpy as jnp
import numpy as np
from jax import lax
from jax.experimental import pallas as pl
from jax.experimental.pallas import tpu as pltpu
from jax.sharding import PartitionSpec as P

theta_base = 500000.0
piece = 256
MESH = pl.DeviceIdType.MESH
QUERY, OUT = 0, 1
BY_X, BY_Y, CORE_X, CORE_Y = range(4)


def rotary_tables(rows, blocks, head_size):
    middle = head_size // 2
    freq = theta_base ** (-2.0 * np.arange(middle, dtype=np.float64) / head_size)
    freq = np.concatenate([freq, freq])[None, :]
    sign = np.where(np.arange(head_size) < middle, -1.0, 1.0)[None, :]

    def tables(positions):
        angles = positions[:, None].astype(np.float64) * freq
        return np.cos(angles).astype(np.float32), (sign * np.sin(angles)).astype(np.float32)

    return tables(np.arange(rows)) + tables(np.arange(blocks) * rows)


def kernel(
    ctx_size, fsdp_size, pieces,
    tok_hbm, wq_hbm, key_hbm, val_hbm, wo_hbm, gates_ref, routes_ref, cos_row, sin_row, cos_blk, sin_blk,
    out_hbm,
    tok, wq, wo, kv, acc, queries, hidden, out_buf,
    send_sem, recv_sem, own_send, own_recv, kv_send, kv_recv, load_sem, wo_load, out_sem,
):
    c = lax.axis_index("ctx")
    f = lax.axis_index("fsdp")
    core = lax.rem(f, 2)
    h = f // 2
    y = lax.rem(c, 2)
    z = c // 2
    chips = fsdp_size // 2
    pairs = ctx_size // 2
    rows = tok.shape[0]
    head_size = kv.shape[2] // 2
    head_count = queries.shape[1] // head_size
    c_mate = z * 2 + (1 - y)
    f_mate = h * 2 + (1 - core)

    def chip_at(d):
        return lax.rem(h + d + chips, chips) * 2 + core

    load_wq = [
        pltpu.make_async_copy(wq_hbm.at[half, s], wq.at[f, half, s], load_sem.at[4 + half * pieces + s])
        for half in range(2)
        for s in range(pieces)
    ]
    load_k = pltpu.make_async_copy(key_hbm, kv.at[c, :, pl.ds(0, head_size)], load_sem.at[0])
    load_v = pltpu.make_async_copy(val_hbm, kv.at[c, :, pl.ds(head_size, head_size)], load_sem.at[1])
    load_tok = pltpu.make_async_copy(tok_hbm, tok, load_sem.at[2])
    load_wo = [
        pltpu.make_async_copy(
            wo_hbm.at[:, pl.ds((half * pieces + s) * piece, piece)],
            wo.at[f, half, s],
            wo_load.at[half * pieces + s],
        )
        for half in range(2)
        for s in range(pieces)
    ]
    load_k.start()
    load_v.start()
    load_tok.start()
    for copy in load_wq + load_wo:
        copy.start()

    barrier = pltpu.get_barrier_semaphore()
    partners = [(c, f_mate), (c_mate, f)]
    partners += [(c, chip_at(d)) for d in range(1, chips)]
    partners += [(lax.rem(z + d, pairs) * 2 + y, f) for d in range(1, pairs)]
    for partner in partners:
        pl.semaphore_signal(barrier, inc=1, device_id=partner, device_id_type=MESH)
    pl.semaphore_wait(barrier, len(partners))

    def remote(src, dst, sem_s, sem_r, device):
        return pltpu.make_async_remote_copy(
            src_ref=src, dst_ref=dst, send_sem=sem_s, recv_sem=sem_r, device_id=device, device_id_type=MESH
        )

    def held(w, g, half, s):
        return (wq if w == QUERY else wo).at[g, half, s]

    def transfer(w, kind, d, s):
        g = chip_at(-d)
        sems = (send_sem.at[w, kind, d - 1, s], recv_sem.at[w, kind, d - 1, s])
        if kind == BY_X:
            here = wq_hbm.at[y, s] if w == QUERY else held(w, f, y, s)
            return remote(here, held(w, f, y, s), *sems, (c, chip_at(d)))
        half = y if kind == CORE_X or kind == BY_Y else 1 - y
        block = held(w, g, half, s)
        return remote(block, block, *sems, (c_mate, f) if kind == BY_Y else (c, f_mate))

    own_wq = [
        remote(wq_hbm.at[half], wq.at[f, half], own_send.at[QUERY, half], own_recv.at[QUERY, half], (c, f_mate))
        for half in range(2)
    ]
    own_wo = [
        remote(wo.at[f, half], wo.at[f, half], own_send.at[OUT, half], own_recv.at[OUT, half], (c, f_mate))
        for half in range(2)
    ]

    started = []

    def start(copy):
        copy.start()
        started.append(copy)

    stream = [(w, s) for w in (QUERY, OUT) for s in range(pieces)]

    def send_x(position):
        if position < len(stream):
            for d in range(1, chips):
                start(transfer(stream[position][0], BY_X, d, stream[position][1]))

    send_x(0)
    load_k.wait()
    load_v.wait()
    kv_mate = remote(kv.at[c], kv.at[c], kv_send.at[0, 0], kv_recv.at[c], (c_mate, f))
    kv_mate.start()
    for copy in own_wq:
        copy.start()
    for copy in load_wo:
        copy.wait()
    send_x(1)

    def kv_copy(which, block, zz):
        return remote(kv.at[block], kv.at[block], kv_send.at[which, zz], kv_recv.at[block], (zz * 2 + y, f))

    def kv_wait(block):
        remote(kv.at[block], kv.at[block], kv_send.at[0, 0], kv_recv.at[block], (c_mate, f)).wait_recv()

    def kv_spread(which, block):
        for zz in range(1, pairs):
            @pl.when(zz > z)
            def _():
                kv_copy(which, block, zz).start()

    kv_spread(0, c)

    def project(g, half, s, count):
        width = count * piece
        at = pl.multiple_of(((g * 2 + half) * pieces + s) * piece, piece)
        weight = wq[g, half, pl.ds(s, count)].reshape(width, acc.shape[1])
        return jnp.dot(tok[:, pl.ds(at, width)], weight, preferred_element_type=jnp.float32)

    load_tok.wait()
    for copy in load_wq:
        copy.wait()
    acc[...] = project(f, 0, 0, pieces)
    acc[...] += project(f, 1, 0, pieces)
    kv_wait(c_mate)
    kv_spread(1, c_mate)
    for half in range(2):
        own_wq[half].wait_recv()
        acc[...] += project(f_mate, half, 0, pieces)

    def arrive_x(w, s):
        for d in range(1, chips):
            transfer(w, BY_X, d, s).wait_recv()
            start(transfer(w, BY_Y, d, s))
            start(transfer(w, CORE_X, d, s))
        send_x(w * pieces + s + 2)

    def arrive_y(w, s):
        for d in range(1, chips):
            g = chip_at(-d)
            block = held(w, g, 1 - y, s)
            remote(
                block, block, send_sem.at[w, BY_Y, d - 1, s], recv_sem.at[w, BY_Y, d - 1, s], (c_mate, f)
            ).wait_recv()
            start(transfer(w, CORE_Y, d, s))

    def wait_piece(w, kind, d, s):
        g = lax.rem(h - d + chips, chips) * 2 + (1 - core)
        half = y if kind == CORE_X else 1 - y
        block = held(w, g, half, s)
        remote(
            block, block, send_sem.at[w, kind, d - 1, s], recv_sem.at[w, kind, d - 1, s], (c, f_mate)
        ).wait_recv()
        return g, half

    for t in range(pieces + 1):
        if t < pieces:
            arrive_x(QUERY, t)
        if t == pieces:
            arrive_x(OUT, 0)
        if t >= 1:
            arrive_y(QUERY, t - 1)
        if t < pieces:
            for d in range(1, chips):
                acc[...] += project(chip_at(-d), y, t, 1)
        if t >= 1:
            for d in range(1, chips):
                acc[...] += project(chip_at(-d), 1 - y, t - 1, 1)
            for d in range(1, chips):
                g, half = wait_piece(QUERY, CORE_X, d, t - 1)
                acc[...] += project(g, half, t - 1, 1)
        if t >= 2:
            for d in range(1, chips):
                g, half = wait_piece(QUERY, CORE_Y, d, t - 2)
                acc[...] += project(g, half, t - 2, 1)
    for d in range(1, chips):
        g, half = wait_piece(QUERY, CORE_Y, d, pieces - 1)
        acc[...] += project(g, half, pieces - 1, 1)
    for copy in own_wo:
        copy.start()

    cos_c, sin_c = cos_blk[pl.ds(c, 1), :], sin_blk[pl.ds(c, 1), :]
    cosine = cos_row[...] * cos_c - sin_row[...] * sin_c
    signed_sine = sin_row[...] * cos_c + cos_row[...] * sin_c
    for n in range(head_count):
        part = acc[:, n * head_size : (n + 1) * head_size]
        turned = part * cosine + pltpu.roll(part, head_size // 2, 1) * signed_sine
        queries[:, n * head_size : (n + 1) * head_size] = turned.astype(jnp.bfloat16)

    @pl.loop(0, z * 2)
    def _(block):
        kv_wait(block)

    to_log2 = float(head_size ** -0.5 * np.log2(np.e))
    gains = gates_ref[...].astype(jnp.float32)
    picks = routes_ref[...]

    def attend(n):
        q = queries[:, n * head_size : (n + 1) * head_size]

        def score(block):
            return (
                lax.dot_general(
                    q, kv[block, :, :head_size], (((1,), (1,)), ((), ())), preferred_element_type=jnp.float32
                )
                * to_log2
            )

        def weigh(block, terms):
            return jnp.dot(
                terms.astype(jnp.bfloat16), kv[block, :, head_size:], preferred_element_type=jnp.float32
            )

        own = score(c)
        row = lax.broadcasted_iota(jnp.int32, own.shape, 0)
        col = lax.broadcasted_iota(jnp.int32, own.shape, 1)
        own = jnp.where(col <= row, own, -1e30)
        top = jnp.max(own, axis=1, keepdims=True)
        terms = jnp.exp2(own - top)

        def step(block, carried):
            top, total, mix = carried
            here = score(block)
            new_top = jnp.maximum(top, jnp.max(here, axis=1, keepdims=True))
            factor = jnp.exp2(top - new_top)
            terms = jnp.exp2(here - new_top)
            total = total * factor + jnp.sum(terms, axis=1, keepdims=True)
            return new_top, total, mix * factor + weigh(block, terms)

        top, total, mix = lax.fori_loop(
            0, c, step, (top, jnp.sum(terms, axis=1, keepdims=True), weigh(c, terms))
        )
        if n == 0:
            gain = gains[:, 0:1]
        else:
            gain = jnp.where(picks[:, 0:1] + 1 == n, gains[:, 1:2], 0.0) + jnp.where(
                picks[:, 1:2] + 1 == n, gains[:, 2:3], 0.0
            )
        hidden[:, n * head_size : (n + 1) * head_size] = (mix / total * gain).astype(jnp.bfloat16)

    def serve(t):
        if t < pieces:
            arrive_x(OUT, t)
        if 1 <= t <= pieces:
            arrive_y(OUT, t - 1)

    served = 1
    for n in range(head_count):
        attend(n)
        if n % 2 == 1 and served <= pieces:
            serve(served)
            served += 1

    def emit(g, half, s):
        result = jnp.dot(hidden[...], wo[g, half, s], preferred_element_type=jnp.float32)
        at = pl.multiple_of(((g * 2 + half) * pieces + s) * piece, piece)
        out_buf[g, half, s] = result.astype(jnp.bfloat16)
        pltpu.make_async_copy(
            out_buf.at[g, half, s], out_hbm.at[:, pl.ds(at, piece)], out_sem.at[g, half, s]
        ).start()

    for half in range(2):
        for s in range(pieces):
            emit(f, half, s)
    for half in range(2):
        own_wo[half].wait_recv()
        for s in range(pieces):
            emit(f_mate, half, s)

    for t in range(pieces + 2):
        if t >= served:
            serve(t)
        for d in range(1, chips):
            if t < pieces:
                emit(chip_at(-d), y, t)
            if 1 <= t <= pieces:
                emit(chip_at(-d), 1 - y, t - 1)
                g, half = wait_piece(OUT, CORE_X, d, t - 1)
                emit(g, half, t - 1)
            if t >= 2:
                g, half = wait_piece(OUT, CORE_Y, d, t - 2)
                emit(g, half, t - 2)

    for copy in started + own_wq + own_wo + [kv_mate]:
        copy.wait_send()
    for which, block in ((0, c), (1, c_mate)):
        for zz in range(1, pairs):
            @pl.when(zz > z)
            def _():
                kv_copy(which, block, zz).wait_send()
    for g in range(fsdp_size):
        for half in range(2):
            for s in range(pieces):
                at = ((g * 2 + half) * pieces + s) * piece
                pltpu.make_async_copy(
                    out_buf.at[g, half, s], out_hbm.at[:, pl.ds(at, piece)], out_sem.at[g, half, s]
                ).wait()


def per_device(ctx_size, fsdp_size, tokens, w_query, keys, values, gates, routes, w_out):
    rows, width = tokens.shape[1:]
    depth, inner = w_query.shape
    head_size = keys.shape[2]
    pieces = depth // (2 * piece)
    chips = fsdp_size // 2
    pairs = ctx_size // 2
    tables = [jnp.asarray(t) for t in rotary_tables(rows, ctx_size, head_size)]
    anywhere = pl.BlockSpec(memory_space=pl.ANY)
    in_vmem = pl.BlockSpec(memory_space=pltpu.VMEM)
    bf16 = jnp.bfloat16
    dma = pltpu.SemaphoreType.DMA
    mixed = pl.pallas_call(
        functools.partial(kernel, ctx_size, fsdp_size, pieces),
        out_shape=jax.ShapeDtypeStruct((rows, width), bf16),
        in_specs=[anywhere] * 5 + [in_vmem] * 6,
        out_specs=anywhere,
        scratch_shapes=[
            pltpu.VMEM((rows, width), bf16),
            pltpu.VMEM((fsdp_size, 2, pieces, piece, inner), bf16),
            pltpu.VMEM((fsdp_size, 2, pieces, inner, piece), bf16),
            pltpu.VMEM((ctx_size, rows, 2 * head_size), bf16),
            pltpu.VMEM((rows, inner), jnp.float32),
            pltpu.VMEM((rows, inner), bf16),
            pltpu.VMEM((rows, inner), bf16),
            pltpu.VMEM((fsdp_size, 2, pieces, rows, piece), bf16),
            dma((2, 4, chips - 1, pieces)),
            dma((2, 4, chips - 1, pieces)),
            dma((2, 2)),
            dma((2, 2)),
            dma((2, pairs)),
            dma((ctx_size,)),
            dma((4 + 2 * pieces,)),
            dma((2 * pieces,)),
            dma((fsdp_size, 2, pieces)),
        ],
        compiler_params=pltpu.CompilerParams(
            collective_id=0, has_side_effects=True, vmem_limit_bytes=50 * 1024 * 1024
        ),
    )(
        tokens[0],
        w_query.reshape(2, pieces, piece, inner),
        keys[0],
        values[0],
        w_out,
        gates[0],
        routes[0],
        *tables,
    )
    return mixed[None]


def solution(mesh):
    in_specs = (
        P("fsdp", "ctx", None),
        P("fsdp", None),
        P("fsdp", "ctx", None),
        P("fsdp", "ctx", None),
        P("fsdp", "ctx", None),
        P("fsdp", "ctx", None),
        P(None, "fsdp"),
    )
    return jax.shard_map(
        functools.partial(per_device, mesh.shape["ctx"], mesh.shape["fsdp"]),
        mesh=mesh,
        in_specs=in_specs,
        out_specs=P("fsdp", "ctx", None),
        check_vma=False,
    )
```

time: 226 us -> 78.4 us (0.35)
  the two profiles are of different devices: /device:TPU:28 before, /device:TPU:25 now
where the time goes in v1:
time: 78.4 us; the launch traced here: 78 us
  Pallas kernels  65.3 us (83%)
  local copies, waits for them, and re-layouts  12.7 us (16%)
    pallas_call x1, Pallas kernels, per_device(): pl.pallas_call(functools.partial(kernel, ctx_size, fsdp_size, pieces), ou...  65.3 us
    unnamed x17, local copies, waits for them, and re-layouts  12.7 us

profile of v1, /device:TPU:25, one launch (start us, length us, event | category | flops | bytes accessed | tf_op | source)
XLA Modules:
  0.0 78.0 jit_solution(6225495891026358115)
XLA Ops:
  0.0 0.8 %copy.12 = bf16[1,256,3]{2,1,0:T(8,128)(2,1)S(1)} copy(bf16[1,256,3]{1,2,0:T(4,128)(2,1)} %param.15) | data formatting | bytes 3072 | tf_op args[4]
  0.8 0.8 %copy.13 = s32[1,256,2]{2,1,0:T(8,128)S(1)} copy(s32[1,256,2]{1,2,0:T(2,128)} %param.16) | data formatting | bytes 4096 | tf_op args[5]
  1.6 0.0 copy-start
  1.6 1.6 %copy-done = bf16[2048,512]{1,0:T(8,128)(2,1)S(1)} copy-done((bf16[2048,512]{1,0:T(8,128)(2,1)S(1)}, bf16[2048,512]{1,0:T(8,128)(2,1)}, u32[]{:S(2)}) %copy-start) | copy-done | bytes 2097176
  3.2 0.0 copy-start.1
  3.2 0.9 %copy-done.1 = f32[256,128]{1,0:T(8,128)S(1)} copy-done((f32[256,128]{1,0:T(8,128)S(1)}, f32[256,128]{1,0:T(8,128)}, u32[]{:S(2)}) %copy-start.1) | copy-done | bytes 131096
  4.1 0.0 copy-start.2
  4.1 0.9 %copy-done.2 = f32[256,128]{1,0:T(8,128)S(1)} copy-done((f32[256,128]{1,0:T(8,128)S(1)}, f32[256,128]{1,0:T(8,128)}, u32[]{:S(2)}) %copy-start.2) | copy-done | bytes 131096
  5.0 0.0 copy-start.3
  5.0 0.8 %copy-done.3 = bf16[1,256,128]{2,1,0:T(8,128)(2,1)S(1)} copy-done((bf16[1,256,128]{2,1,0:T(8,128)(2,1)S(1)}, bf16[1,256,128]{2,1,0:T(8,128)(2,1)}, u32[]{:S(2)}) %copy-start.3) | copy-done | bytes 65560
  5.9 0.0 copy-start.4
  5.9 0.8 %copy-done.4 = bf16[1,256,128]{2,1,0:T(8,128)(2,1)S(1)} copy-done((bf16[1,256,128]{2,1,0:T(8,128)(2,1)S(1)}, bf16[1,256,128]{2,1,0:T(8,128)(2,1)}, u32[]{:S(2)}) %copy-start.4) | copy-done | bytes 65560
  6.7 0.0 copy-start.5
  6.7 0.7 copy-done.5
  7.4 0.0 copy-start.6
  7.4 0.7 copy-done.6
  8.1 65.3 %shard_map.109 = bf16[256,8192]{1,0:T(8,128)(2,1)} custom-call(bf16[256,8192]{1,0:T(8,128)(2,1)} %bitcast.13, bf16[2,4,256,512]{3,2,1,0:T(8,128)(2,1)S(1)} %bitcast.7, bf16[256,128]{1,0:T(8,128)(2,1)S(1)} %bitcast.10, bf16[256,128]{1,0:T(8,128)(2,1)S(1)} %bitcast.11, bf16[512,2048]{1,0:T(8,128)(2,1)} %wo_hbm.1, bf16[256,3]{1,0:T(8,128)(2,1)S(1)} %bitcast.9, ...), custom_call_target="tpu_custom_call" | custom-call | tf_op jit(solution)/shard_map/pallas_call | solution.py:349
  73.4 4.6 %copy.15 = bf16[1,256,8192]{2,1,0:T(8,128)(2,1)} copy(bf16[1,256,8192]{2,1,0:T(8,128)(2,1)} %bitcast.12) | data formatting | bytes 8388608
Async XLA Ops:
  1.6 1.6 %copy-start = (bf16[2048,512]{1,0:T(8,128)(2,1)S(1)}, bf16[2048,512]{1,0:T(8,128)(2,1)}, u32[]{:S(2)}) copy-start(bf16[2048,512]{1,0:T(8,128)(2,1)} %param.12) | copy-start | bytes 6291460
  3.2 0.9 %copy-start.1 = (f32[256,128]{1,0:T(8,128)S(1)}, f32[256,128]{1,0:T(8,128)}, u32[]{:S(2)}) copy-start(f32[256,128]{1,0:T(8,128)} %constant.9.clone.sin_row) | copy-start | bytes 393220
  4.1 0.9 %copy-start.2 = (f32[256,128]{1,0:T(8,128)S(1)}, f32[256,128]{1,0:T(8,128)}, u32[]{:S(2)}) copy-start(f32[256,128]{1,0:T(8,128)} %constant.8.clone.cos_row) | copy-start | bytes 393220
  5.0 0.8 %copy-start.3 = (bf16[1,256,128]{2,1,0:T(8,128)(2,1)S(1)}, bf16[1,256,128]{2,1,0:T(8,128)(2,1)}, u32[]{:S(2)}) copy-start(bf16[1,256,128]{2,1,0:T(8,128)(2,1)} %param.13) | copy-start | bytes 196612
  5.9 0.8 %copy-start.4 = (bf16[1,256,128]{2,1,0:T(8,128)(2,1)S(1)}, bf16[1,256,128]{2,1,0:T(8,128)(2,1)}, u32[]{:S(2)}) copy-start(bf16[1,256,128]{2,1,0:T(8,128)(2,1)} %param.14) | copy-start | bytes 196612
  6.7 0.7 copy-start.5
  7.4 0.7 copy-start.6

commit v2 on v1

--- a/solution.py
+++ b/solution.py
@@ -12,7 +12,7 @@
 piece = 256
 MESH = pl.DeviceIdType.MESH
 QUERY, OUT = 0, 1
-BY_X, BY_Y, CORE_X, CORE_Y = range(4)
+BY_X, BY_Y, CORE_X, CORE_Y, BY_ZX, BY_ZY, CORE_ZX, CORE_ZY = range(8)
 
 
 def rotary_tables(rows, blocks, head_size):
@@ -23,17 +23,18 @@
 
     def tables(positions):
         angles = positions[:, None].astype(np.float64) * freq
-        return np.cos(angles).astype(np.float32), (sign * np.sin(angles)).astype(np.float32)
-
-    return tables(np.arange(rows)) + tables(np.arange(blocks) * rows)
+        sine = np.sin(angles)
+        return np.stack([np.cos(angles), sign * sine, sine]).astype(np.float32)
+
+    return tables(np.arange(rows)), tables(np.arange(blocks) * rows)
 
 
 def kernel(
     ctx_size, fsdp_size, pieces,
-    tok_hbm, wq_hbm, key_hbm, val_hbm, wo_hbm, gates_ref, routes_ref, cos_row, sin_row, cos_blk, sin_blk,
+    tok_hbm, wq_hbm, key_hbm, val_hbm, wo_hbm, gates_ref, routes_hbm, row_hbm, blk_hbm,
     out_hbm,
-    tok, wq, wo, kv, acc, queries, hidden, out_buf,
-    send_sem, recv_sem, own_send, own_recv, kv_send, kv_recv, load_sem, wo_load, out_sem,
+    routes_ref, row_tab, blk_tab, tok, wq, wo, kv, acc, queries, hidden, out_buf,
+    send_sem, recv_sem, own_send, own_recv, kv_send, kv_recv, load_sem, wo_load, out_sem, small_sem,
 ):
     c = lax.axis_index("ctx")
     f = lax.axis_index("fsdp")
@@ -48,6 +49,12 @@
     head_count = queries.shape[1] // head_size
     c_mate = z * 2 + (1 - y)
     f_mate = h * 2 + (1 - core)
+    cube = pieces == 4 and pairs % 2 == 0
+    z_bit = lax.rem(z, 2)
+    c_next = (z + 1 - 2 * z_bit) * 2 + y
+    roots = [2 + z_bit, 0, 1] if cube else list(range(pieces))
+    steps = len(roots)
+    z_root = 3 - z_bit
 
     def chip_at(d):
         return lax.rem(h + d + chips, chips) * 2 + core
@@ -69,10 +76,16 @@
         for half in range(2)
         for s in range(pieces)
     ]
+    small = [
+        pltpu.make_async_copy(source, target, small_sem.at[i])
+        for i, (source, target) in enumerate(
+            ((routes_hbm, routes_ref), (row_hbm, row_tab), (blk_hbm, blk_tab))
+        )
+    ]
     load_k.start()
     load_v.start()
     load_tok.start()
-    for copy in load_wq + load_wo:
+    for copy in load_wq + load_wo + small:
         copy.start()
 
     barrier = pltpu.get_barrier_semaphore()
@@ -91,15 +104,32 @@
     def held(w, g, half, s):
         return (wq if w == QUERY else wo).at[g, half, s]
 
-    def transfer(w, kind, d, s):
-        g = chip_at(-d)
-        sems = (send_sem.at[w, kind, d - 1, s], recv_sem.at[w, kind, d - 1, s])
+    def transfer(w, kind, d, t):
+        s = z_root if kind in (CORE_ZX, CORE_ZY) else roots[t]
+        sems = (send_sem.at[w, kind, d - 1, t], recv_sem.at[w, kind, d - 1, t])
         if kind == BY_X:
             here = wq_hbm.at[y, s] if w == QUERY else held(w, f, y, s)
             return remote(here, held(w, f, y, s), *sems, (c, chip_at(d)))
-        half = y if kind == CORE_X or kind == BY_Y else 1 - y
+        half = y if kind in (BY_Y, CORE_X, BY_ZX, CORE_ZX) else 1 - y
+        block = held(w, chip_at(-d), half, s)
+        if kind == BY_Y:
+            target = (c_mate, f)
+        elif kind in (BY_ZX, BY_ZY):
+            target = (c_next, f)
+        else:
+            target = (c, f_mate)
+        return remote(block, block, *sems, target)
+
+    def arrival(w, kind, d, t):
+        s = z_root if kind in (BY_ZX, BY_ZY, CORE_ZX, CORE_ZY) else roots[t]
+        from_core = kind in (CORE_X, CORE_Y, CORE_ZX, CORE_ZY)
+        g = lax.rem(h - d + chips, chips) * 2 + ((1 - core) if from_core else core)
+        half = y if kind in (BY_X, CORE_X, BY_ZX, CORE_ZX) else 1 - y
         block = held(w, g, half, s)
-        return remote(block, block, *sems, (c_mate, f) if kind == BY_Y else (c, f_mate))
+        remote(
+            block, block, send_sem.at[w, kind, d - 1, t], recv_sem.at[w, kind, d - 1, t], (c, f_mate)
+        ).wait_recv()
+        return g, half, s
 
     own_wq = [
         remote(wq_hbm.at[half], wq.at[f, half], own_send.at[QUERY, half], own_recv.at[QUERY, half], (c, f_mate))
@@ -116,7 +146,7 @@
         copy.start()
         started.append(copy)
 
-    stream = [(w, s) for w in (QUERY, OUT) for s in range(pieces)]
+    stream = [(w, s) for w in (QUERY, OUT) for s in range(steps)]
 
     def send_x(position):
         if position < len(stream):
@@ -159,66 +189,64 @@
         copy.wait()
     acc[...] = project(f, 0, 0, pieces)
     acc[...] += project(f, 1, 0, pieces)
-    kv_wait(c_mate)
-    kv_spread(1, c_mate)
     for half in range(2):
         own_wq[half].wait_recv()
         acc[...] += project(f_mate, half, 0, pieces)
 
-    def arrive_x(w, s):
+    def come(w, kind, t, forwards):
+        landed = []
         for d in range(1, chips):
-            transfer(w, BY_X, d, s).wait_recv()
-            start(transfer(w, BY_Y, d, s))
-            start(transfer(w, CORE_X, d, s))
-        send_x(w * pieces + s + 2)
-
-    def arrive_y(w, s):
-        for d in range(1, chips):
-            g = chip_at(-d)
-            block = held(w, g, 1 - y, s)
-            remote(
-                block, block, send_sem.at[w, BY_Y, d - 1, s], recv_sem.at[w, BY_Y, d - 1, s], (c_mate, f)
-            ).wait_recv()
-            start(transfer(w, CORE_Y, d, s))
-
-    def wait_piece(w, kind, d, s):
-        g = lax.rem(h - d + chips, chips) * 2 + (1 - core)
-        half = y if kind == CORE_X else 1 - y
-        block = held(w, g, half, s)
-        remote(
-            block, block, send_sem.at[w, kind, d - 1, s], recv_sem.at[w, kind, d - 1, s], (c, f_mate)
-        ).wait_recv()
-        return g, half
-
-    for t in range(pieces + 1):
-        if t < pieces:
-            arrive_x(QUERY, t)
-        if t == pieces:
-            arrive_x(OUT, 0)
-        if t >= 1:
-            arrive_y(QUERY, t - 1)
-        if t < pieces:
-            for d in range(1, chips):
-                acc[...] += project(chip_at(-d), y, t, 1)
-        if t >= 1:
-            for d in range(1, chips):
-                acc[...] += project(chip_at(-d), 1 - y, t - 1, 1)
-            for d in range(1, chips):
-                g, half = wait_piece(QUERY, CORE_X, d, t - 1)
-                acc[...] += project(g, half, t - 1, 1)
-        if t >= 2:
-            for d in range(1, chips):
-                g, half = wait_piece(QUERY, CORE_Y, d, t - 2)
-                acc[...] += project(g, half, t - 2, 1)
-    for d in range(1, chips):
-        g, half = wait_piece(QUERY, CORE_Y, d, pieces - 1)
-        acc[...] += project(g, half, pieces - 1, 1)
+            landed.append(arrival(w, kind, d, t))
+            for onward in forwards:
+                start(transfer(w, onward, d, t))
+        return landed
+
+    def serve(w, t):
+        landed = []
+        if t < steps:
+            landed += come(w, BY_X, t, ([BY_ZX] if cube and t == 0 else []) + [BY_Y, CORE_X])
+            send_x(w * steps + t + 2)
+        if 1 <= t <= steps:
+            landed += come(w, BY_Y, t - 1, ([BY_ZY] if cube and t == 1 else []) + [CORE_Y])
+        if cube and t == 2:
+            landed += come(w, BY_ZX, 0, [CORE_ZX])
+        if cube and t == 3:
+            landed += come(w, BY_ZY, 0, [CORE_ZY])
+        return landed
+
+    def gather_core(w, t):
+        landed = []
+        t -= 1
+        if 0 <= t < steps:
+            landed += come(w, CORE_X, t, [])
+        if 1 <= t <= steps:
+            landed += come(w, CORE_Y, t - 1, [])
+        if cube and t == 2:
+            landed += come(w, CORE_ZX, 0, [])
+        if cube and t == 3:
+            landed += come(w, CORE_ZY, 0, [])
+        return landed
+
+    for t in range(steps + 2):
+        landed = serve(QUERY, t)
+        if t == steps:
+            out_landed = serve(OUT, 0)
+        if t == min(1, steps):
+            kv_wait(c_mate)
+            kv_spread(1, c_mate)
+        for g, half, s in landed:
+            acc[...] += project(g, half, s, 1)
+        for g, half, s in gather_core(QUERY, t):
+            acc[...] += project(g, half, s, 1)
     for copy in own_wo:
         copy.start()
 
-    cos_c, sin_c = cos_blk[pl.ds(c, 1), :], sin_blk[pl.ds(c, 1), :]
-    cosine = cos_row[...] * cos_c - sin_row[...] * sin_c
-    signed_sine = sin_row[...] * cos_c + cos_row[...] * sin_c
+    for copy in small:
+        copy.wait()
+    cos_c, sin_c = blk_tab[0, pl.ds(c, 1), :], blk_tab[1, pl.ds(c, 1), :]
+    plain_c = blk_tab[2, pl.ds(c, 1), :]
+    cosine = row_tab[0] * cos_c - row_tab[2] * plain_c
+    signed_sine = row_tab[1] * cos_c + row_tab[0] * sin_c
     for n in range(head_count):
         part = acc[:, n * head_size : (n + 1) * head_size]
         turned = part * cosine + pltpu.roll(part, head_size // 2, 1) * signed_sine
@@ -231,6 +259,13 @@
     to_log2 = float(head_size ** -0.5 * np.log2(np.e))
     gains = gates_ref[...].astype(jnp.float32)
     picks = routes_ref[...]
+    by_head = [gains[0:1, :]] + [
+        jnp.where(picks[0:1, :] + 1 == n, gains[1:2, :], 0.0)
+        + jnp.where(picks[1:2, :] + 1 == n, gains[2:3, :], 0.0)
+        for n in range(1, head_count)
+    ]
+    by_head += [jnp.zeros_like(by_head[0])] * (8 - head_count)
+    mixing = jnp.concatenate(by_head, axis=0).T
 
     def attend(n):
         q = queries[:, n * head_size : (n + 1) * head_size]
@@ -267,25 +302,14 @@
         top, total, mix = lax.fori_loop(
             0, c, step, (top, jnp.sum(terms, axis=1, keepdims=True), weigh(c, terms))
         )
-        if n == 0:
-            gain = gains[:, 0:1]
-        else:
-            gain = jnp.where(picks[:, 0:1] + 1 == n, gains[:, 1:2], 0.0) + jnp.where(
-                picks[:, 1:2] + 1 == n, gains[:, 2:3], 0.0
-            )
+        gain = mixing[:, n : n + 1]
         hidden[:, n * head_size : (n + 1) * head_size] = (mix / total * gain).astype(jnp.bfloat16)
-
-    def serve(t):
-        if t < pieces:
-            arrive_x(OUT, t)
-        if 1 <= t <= pieces:
-            arrive_y(OUT, t - 1)
 
     served = 1
     for n in range(head_count):
         attend(n)
-        if n % 2 == 1 and served <= pieces:
-            serve(served)
+        if n % 2 == 1 and served <= steps:
+            out_landed += serve(OUT, served)
             served += 1
 
     def emit(g, half, s):
@@ -304,19 +328,14 @@
         for s in range(pieces):
             emit(f_mate, half, s)
 
-    for t in range(pieces + 2):
+    for t in range(steps + 2):
         if t >= served:
-            serve(t)
-        for d in range(1, chips):
-            if t < pieces:
-                emit(chip_at(-d), y, t)
-            if 1 <= t <= pieces:
-                emit(chip_at(-d), 1 - y, t - 1)
-                g, half = wait_piece(OUT, CORE_X, d, t - 1)
-                emit(g, half, t - 1)
-            if t >= 2:
-                g, half = wait_piece(OUT, CORE_Y, d, t - 2)
-                emit(g, half, t - 2)
+            out_landed = serve(OUT, t)
+        if t >= served - 1:
+            for g, half, s in out_landed:
+                emit(g, half, s)
+        for g, half, s in gather_core(OUT, t):
+            emit(g, half, s)
 
     for copy in started + own_wq + own_wo + [kv_mate]:
         copy.wait_send()
@@ -343,15 +362,17 @@
     pairs = ctx_size // 2
     tables = [jnp.asarray(t) for t in rotary_tables(rows, ctx_size, head_size)]
     anywhere = pl.BlockSpec(memory_space=pl.ANY)
-    in_vmem = pl.BlockSpec(memory_space=pltpu.VMEM)
     bf16 = jnp.bfloat16
     dma = pltpu.SemaphoreType.DMA
     mixed = pl.pallas_call(
         functools.partial(kernel, ctx_size, fsdp_size, pieces),
         out_shape=jax.ShapeDtypeStruct((rows, width), bf16),
-        in_specs=[anywhere] * 5 + [in_vmem] * 6,
+        in_specs=[anywhere] * 5 + [pl.BlockSpec(memory_space=pltpu.VMEM)] + [anywhere] * 3,
         out_specs=anywhere,
         scratch_shapes=[
+            pltpu.VMEM((routes.shape[2], rows), jnp.int32),
+            pltpu.VMEM(tables[0].shape, jnp.float32),
+            pltpu.VMEM(tables[1].shape, jnp.float32),
             pltpu.VMEM((rows, width), bf16),
             pltpu.VMEM((fsdp_size, 2, pieces, piece, inner), bf16),
             pltpu.VMEM((fsdp_size, 2, pieces, inner, piece), bf16),
@@ -360,8 +381,8 @@
             pltpu.VMEM((rows, inner), bf16),
             pltpu.VMEM((rows, inner), bf16),
             pltpu.VMEM((fsdp_size, 2, pieces, rows, piece), bf16),
-            dma((2, 4, chips - 1, pieces)),
-            dma((2, 4, chips - 1, pieces)),
+            dma((2, 8, chips - 1, pieces)),
+            dma((2, 8, chips - 1, pieces)),
             dma((2, 2)),
             dma((2, 2)),
             dma((2, pairs)),
@@ -369,9 +390,10 @@
             dma((4 + 2 * pieces,)),
             dma((2 * pieces,)),
             dma((fsdp_size, 2, pieces)),
+            dma((3,)),
         ],
         compiler_params=pltpu.CompilerParams(
-            collective_id=0, has_side_effects=True, vmem_limit_bytes=50 * 1024 * 1024
+            collective_id=0, has_side_effects=True, vmem_limit_bytes=62 * 1024 * 1024
         ),
     )(
         tokens[0],
@@ -379,8 +401,8 @@
         keys[0],
         values[0],
         w_out,
-        gates[0],
-        routes[0],
+        gates[0].T,
+        routes[0].T,
         *tables,
     )
     return mixed[None]

time: 78.4 us -> 66 us (0.84)
  the two profiles are of different devices: /device:TPU:25 before, /device:TPU:27 now
where the time goes in v2:
time: 66 us; the launch traced here: 65.8 us
  Pallas kernels  61.2 us (93%)
  local copies, waits for them, and re-layouts  4.64 us (7%)
    pallas_call x1, Pallas kernels, per_device(): pl.pallas_call(functools.partial(kernel, ctx_size, fsdp_size, pieces), ou...  61.2 us
    unnamed x1, local copies, waits for them, and re-layouts  4.64 us

profile of v2, /device:TPU:27, one launch (start us, length us, event | category | flops | bytes accessed | tf_op | source)
XLA Modules:
  0.0 65.8 jit_solution(6487080448556219304)
XLA Ops:
  0.0 61.2 %shard_map.91 = bf16[256,8192]{1,0:T(8,128)(2,1)} custom-call(bf16[256,8192]{1,0:T(8,128)(2,1)} %bitcast.12, bf16[2,4,256,512]{3,2,1,0:T(8,128)(2,1)} %bitcast.13, bf16[256,128]{1,0:T(8,128)(2,1)} %bitcast.14, bf16[256,128]{1,0:T(8,128)(2,1)} %bitcast.15, bf16[512,2048]{1,0:T(8,128)(2,1)} %wo_hbm.1, bf16[3,256]{1,0:T(4,128)(2,1)} %bitcast.16, ...), custom_call_target="tpu_custom_call" | custom-call | tf_op jit(solution)/shard_map/pallas_call | solution.py:367
  61.2 4.6 %copy.11 = bf16[1,256,8192]{2,1,0:T(8,128)(2,1)} copy(bf16[1,256,8192]{2,1,0:T(8,128)(2,1)} %bitcast.11) | data formatting | bytes 8388608

commit v3 on v2

--- a/solution.py
+++ b/solution.py
@@ -171,7 +171,7 @@
         remote(kv.at[block], kv.at[block], kv_send.at[0, 0], kv_recv.at[block], (c_mate, f)).wait_recv()
 
     def kv_spread(which, block):
-        for zz in range(1, pairs):
+        for zz in reversed(range(1, pairs)):
             @pl.when(zz > z)
             def _():
                 kv_copy(which, block, zz).start()
@@ -184,6 +184,8 @@
         weight = wq[g, half, pl.ds(s, count)].reshape(width, acc.shape[1])
         return jnp.dot(tok[:, pl.ds(at, width)], weight, preferred_element_type=jnp.float32)
 
+    kv_wait(c_mate)
+    kv_spread(1, c_mate)
     load_tok.wait()
     for copy in load_wq:
         copy.wait()
@@ -231,9 +233,6 @@
         landed = serve(QUERY, t)
         if t == steps:
             out_landed = serve(OUT, 0)
-        if t == min(1, steps):
-            kv_wait(c_mate)
-            kv_spread(1, c_mate)
         for g, half, s in landed:
             acc[...] += project(g, half, s, 1)
         for g, half, s in gather_core(QUERY, t):

time: 66 us -> 67.7 us (1.026)
  Pallas kernels: 61.2 us -> 62.8 us
    pallas_call x1, Pallas kernels: 61.2 us -> 62.8 us  [per_device(): pl.pallas_call(functools.partial(kernel, ctx_size, fsdp_size, pieces), ou...]
where the time goes in v3:
time: 67.7 us; the launch traced here: 67.5 us
  Pallas kernels  62.8 us (93%)
  local copies, waits for them, and re-layouts  4.64 us (7%)
    pallas_call x1, Pallas kernels, per_device(): pl.pallas_call(functools.partial(kernel, ctx_size, fsdp_size, pieces), ou...  62.8 us
    unnamed x1, local copies, waits for them, and re-layouts  4.64 us

profile of v3, /device:TPU:27, one launch (start us, length us, event | category | flops | bytes accessed | tf_op | source)
XLA Modules:
  0.0 67.5 jit_solution(16702455554756368848)
XLA Ops:
  0.0 62.8 %shard_map.91 = bf16[256,8192]{1,0:T(8,128)(2,1)} custom-call(bf16[256,8192]{1,0:T(8,128)(2,1)} %bitcast.12, bf16[2,4,256,512]{3,2,1,0:T(8,128)(2,1)} %bitcast.13, bf16[256,128]{1,0:T(8,128)(2,1)} %bitcast.14, bf16[256,128]{1,0:T(8,128)(2,1)} %bitcast.15, bf16[512,2048]{1,0:T(8,128)(2,1)} %wo_hbm.1, bf16[3,256]{1,0:T(4,128)(2,1)} %bitcast.16, ...), custom_call_target="tpu_custom_call" | custom-call | tf_op jit(solution)/shard_map/pallas_call | solution.py:366
  62.8 4.6 %copy.11 = bf16[1,256,8192]{2,1,0:T(8,128)(2,1)} copy(bf16[1,256,8192]{2,1,0:T(8,128)(2,1)} %bitcast.11) | data formatting | bytes 8388608

commit v4 on v2

--- a/solution.py
+++ b/solution.py
@@ -252,6 +252,9 @@
         turned = part * cosine + pltpu.roll(part, head_size // 2, 1) * signed_sine
         queries[:, n * head_size : (n + 1) * head_size] = turned.astype(jnp.bfloat16)
 
+    out_landed += serve(OUT, 1)
+    served = 2
+
     @pl.loop(0, z * 2)
     def _(block):
         kv_wait(block)
@@ -305,10 +308,9 @@
         gain = mixing[:, n : n + 1]
         hidden[:, n * head_size : (n + 1) * head_size] = (mix / total * gain).astype(jnp.bfloat16)
 
-    served = 1
     for n in range(head_count):
         attend(n)
-        if n % 2 == 1 and served <= steps:
+        if n == 1 and served <= steps:
             out_landed += serve(OUT, served)
             served += 1
 
@@ -323,16 +325,19 @@
     for half in range(2):
         for s in range(pieces):
             emit(f, half, s)
+    if served <= steps:
+        out_landed += serve(OUT, served)
+        served += 1
     for half in range(2):
         own_wo[half].wait_recv()
         for s in range(pieces):
             emit(f_mate, half, s)
 
+    for g, half, s in out_landed:
+        emit(g, half, s)
     for t in range(steps + 2):
         if t >= served:
-            out_landed = serve(OUT, t)
-        if t >= served - 1:
-            for g, half, s in out_landed:
+            for g, half, s in serve(OUT, t):
                 emit(g, half, s)
         for g, half, s in gather_core(OUT, t):
             emit(g, half, s)

time: 66 us -> 63.2 us (0.958)
  the two profiles are of different devices: /device:TPU:27 before, /device:TPU:28 now
where the time goes in v4:
time: 63.2 us; the launch traced here: 63.1 us
  Pallas kernels  58.4 us (92%)
  local copies, waits for them, and re-layouts  4.64 us (7%)
    pallas_call x1, Pallas kernels, per_device(): pl.pallas_call(functools.partial(kernel, ctx_size, fsdp_size, pieces), ou...  58.4 us
    unnamed x1, local copies, waits for them, and re-layouts  4.64 us

profile of v4, /device:TPU:28, one launch (start us, length us, event | category | flops | bytes accessed | tf_op | source)
XLA Modules:
  0.0 63.1 jit_solution(742820341950689748)
XLA Ops:
  0.0 58.4 %shard_map.91 = bf16[256,8192]{1,0:T(8,128)(2,1)} custom-call(bf16[256,8192]{1,0:T(8,128)(2,1)} %bitcast.12, bf16[2,4,256,512]{3,2,1,0:T(8,128)(2,1)} %bitcast.13, bf16[256,128]{1,0:T(8,128)(2,1)} %bitcast.14, bf16[256,128]{1,0:T(8,128)(2,1)} %bitcast.15, bf16[512,2048]{1,0:T(8,128)(2,1)} %wo_hbm.1, bf16[3,256]{1,0:T(4,128)(2,1)} %bitcast.16, ...), custom_call_target="tpu_custom_call" | custom-call | tf_op jit(solution)/shard_map/pallas_call | solution.py:372
  58.4 4.6 %copy.11 = bf16[1,256,8192]{2,1,0:T(8,128)(2,1)} copy(bf16[1,256,8192]{2,1,0:T(8,128)(2,1)} %bitcast.11) | data formatting | bytes 8388608

commit v5 on v4

--- a/solution.py
+++ b/solution.py
@@ -255,10 +255,6 @@
     out_landed += serve(OUT, 1)
     served = 2
 
-    @pl.loop(0, z * 2)
-    def _(block):
-        kv_wait(block)
-
     to_log2 = float(head_size ** -0.5 * np.log2(np.e))
     gains = gates_ref[...].astype(jnp.float32)
     picks = routes_ref[...]
@@ -293,8 +289,15 @@
         top = jnp.max(own, axis=1, keepdims=True)
         terms = jnp.exp2(own - top)
 
-        def step(block, carried):
+        def step(i, carried):
             top, total, mix = carried
+            block = c - 1 - i
+            if n == 0:
+
+                @pl.when(block < z * 2)
+                def _():
+                    kv_wait(block)
+
             here = score(block)
             new_top = jnp.maximum(top, jnp.max(here, axis=1, keepdims=True))
             factor = jnp.exp2(top - new_top)

time: 63.2 us -> 63.3 us (level)
  no operation moved by 1% of the time
where the time goes in v5:
time: 63.3 us; the launch traced here: 63.1 us
  Pallas kernels  58.5 us (92%)
  local copies, waits for them, and re-layouts  4.64 us (7%)
    pallas_call x1, Pallas kernels, per_device(): pl.pallas_call(functools.partial(kernel, ctx_size, fsdp_size, pieces), ou...  58.5 us
    unnamed x1, local copies, waits for them, and re-layouts  4.64 us

profile of v5, /device:TPU:28, one launch (start us, length us, event | category | flops | bytes accessed | tf_op | source)
XLA Modules:
  0.0 63.1 jit_solution(14977807711000613669)
XLA Ops:
  0.0 58.5 %shard_map.91 = bf16[256,8192]{1,0:T(8,128)(2,1)} custom-call(bf16[256,8192]{1,0:T(8,128)(2,1)} %bitcast.12, bf16[2,4,256,512]{3,2,1,0:T(8,128)(2,1)} %bitcast.13, bf16[256,128]{1,0:T(8,128)(2,1)} %bitcast.14, bf16[256,128]{1,0:T(8,128)(2,1)} %bitcast.15, bf16[512,2048]{1,0:T(8,128)(2,1)} %wo_hbm.1, bf16[3,256]{1,0:T(4,128)(2,1)} %bitcast.16, ...), custom_call_target="tpu_custom_call" | custom-call | tf_op jit(solution)/shard_map/pallas_call | solution.py:375
  58.5 4.6 %copy.11 = bf16[1,256,8192]{2,1,0:T(8,128)(2,1)} copy(bf16[1,256,8192]{2,1,0:T(8,128)(2,1)} %bitcast.11) | data formatting | bytes 8388608
